TPU v7x, 32 devices: a whole 2x2x4 slice. The times are simulated.
32 devices in a mesh: grp: 2 (over y), ex: 4 (over z), lay: 4 (over x, core).
Axes of the slice: x: 2, y: 2, z: 4, core: 2. Of those that a mesh axis runs over, the one named last changes fastest.
Arguments:
- train_grads: bfloat16 [4, 16384, 1024], P('lay', ('grp', 'ex')), parts along dimension 1, may hold values from -0.796875 to 0.796875
- queries: bfloat16 [4, 512, 1024], P('lay', ('grp', 'ex')), parts along dimension 1, may hold values from -0.23925781 to 0.23925781
- out_basis: float32 [4, 32, 32], P('lay'), may hold values from -1 to 1
- in_basis: float32 [4, 32, 32], P('lay'), may hold values from -1 to 1
- eigenvalues: float32 [4, 32, 32], P('lay'), may hold values from 0.05 to 5
Outputs:
- scores: bfloat16 [512, 8192], P('grp', ('ex', 'lay')), parts along dimension 0
There are 2 independent parts, one for each index of `grp`. A program takes and returns all parts, laid end to end along the dimension named above; an argument that names none is the same for every part. Nothing has to cross between parts.
All inputs are finite; a program needn't handle non-finite values.
Results may differ from a plain program's by a relative error of at most 0.0095.
Values may be sent and summed in bfloat16 or wider, within the bound.
A program may use at most 64 MiB of HBM per device.

v0:
```python
import jax
import jax.numpy as jnp
from jax import lax
from jax.sharding import PartitionSpec as P


def condition(grads, out_mat, in_mat, eigen):
    count = grads.shape[0]
    square = grads.astype(jnp.float32).reshape(count, out_mat.shape[0], in_mat.shape[0])
    rotated = jnp.einsum("aj,nab,bk->njk", out_mat, square, in_mat, precision=lax.Precision.HIGHEST)
    damping = 0.1 * jnp.mean(eigen)
    damped = rotated / (eigen + damping)
    restored = jnp.einsum(
        "aj,njk,bk->nab", out_mat, damped, in_mat, precision=lax.Precision.HIGHEST
    )
    return restored.reshape(count, out_mat.shape[0] * in_mat.shape[0]).astype(jnp.bfloat16)


def on_device(train_grads, queries, out_basis, in_basis, eigenvalues):
    conditioned = jnp.stack([condition(queries[0], out_basis[0], in_basis[0], eigenvalues[0])])
    block = jnp.einsum(
        "lqf,ltf->qt",
        lax.all_gather(conditioned, "ex", axis=1, tiled=True),
        train_grads,
        preferred_element_type=jnp.float32,
    )
    return lax.psum_scatter(block.astype(jnp.bfloat16), "lay", scatter_dimension=1, tiled=True)


def solution(mesh):
    placed = (
        P("lay", ("grp", "ex"), None),
        P("lay", ("grp", "ex"), None),
        P("lay", None, None),
        P("lay", None, None),
        P("lay", None, None),
    )
    return jax.shard_map(
        on_device, mesh=mesh, in_specs=placed, out_specs=P("grp", ("ex", "lay")), check_vma=False
    )
```

profile of v0, /device:TPU:0, one launch (start us, length us, event | category | flops | bytes accessed | tf_op | source)
XLA Modules:
  0.0 74.2 jit_solution(17224284626995561774)
XLA Ops:
  6.5 0.0 copy-start
  6.5 0.0 reduce-scatter.2.cloned.1.call-start
  6.5 1.3 %reduce_sum.9 = f32[]{:T(128)} reduce(f32[1,32,32]{2,1,0:T(8,128)} %param.9, f32[]{:T(128)} %constant.2.clone.1), dimensions={0,1,2}, to_apply=%region_0.0 | reduce | flops 1023 | bytes 4104 | tf_op jit(solution)/shard_map/reduce_sum | solution.py:11
  8.5 0.7 add_bitcast_fusion
  9.3 1.1 %copy.7 = bf16[1,64,1024]{1,2,0:T(8,128)(2,1)S(1)} copy(bf16[1,64,1024]{2,1,0:T(8,128)(2,1)} %param.6) | data formatting | bytes 262144 | tf_op args[1]
  10.3 0.9 %copy.8 = bf16[64,32,32]{1,2,0:T(8,128)(2,1)S(1)} copy(bf16[64,32,32]{0,2,1:T(8,128)(2,1)S(1)} %bitcast.29) | data formatting | bytes 262144 | tf_op jit(solution)/shard_map/reshape | solution.py:9
  11.2 0.0 copy-done
  11.2 0.0 copy-start.1
  11.2 2.5 %fusion.10 = f32[64,32,32]{1,2,0:T(8,128)S(1)} fusion(bf16[64,32,32]{1,2,0:T(8,128)(2,1)S(1)} %copy.8, f32[1,32,32]{2,1,0:T(8,128)S(1)} %copy-done), kind=kOutput, calls=%fused_computation.10 | convolution fusion | flops 25165824 | bytes 397312 | tf_op jit(solution)/shard_map/aj,nab,bk->njk/dot_general | solution.py:10
  13.7 1.7 %convolution_divide_fusion = f32[64,32,32]{2,1,0:T(8,128)S(1)} fusion(f32[64,32,32]{1,2,0:T(8,128)S(1)} %fusion.10, f32[32,32]{1,0:T(8,128)S(1)} %add_bitcast_fusion, f32[1,32,32]{2,1,0:T(8,128)} %param.8), kind=kOutput, calls=%fused_computation.3 | convolution fusion | flops 25231360 | bytes 532480 | tf_op jit(solution)/shard_map/aj,nab,bk->njk/dot_general | solution.py:10
  15.4 1.8 %fusion.8 = f32[64,32,32]{2,1,0:T(8,128)S(1)} fusion(f32[64,32,32]{2,1,0:T(8,128)S(1)} %convolution_divide_fusion, f32[1,32,32]{2,1,0:T(8,128)S(1)} %copy-done), kind=kOutput, calls=%fused_computation.8 | convolution fusion | flops 25165824 | bytes 528384 | tf_op jit(solution)/shard_map/aj,njk,bk->nab/dot_general | solution.py:13
  17.2 0.8 %copy.11 = f32[64,32,32]{0,1,2:T(8,128)S(1)} copy(f32[64,32,32]{2,1,0:T(8,128)S(1)} %fusion.8) | data formatting | bytes 524288 | tf_op jit(solution)/shard_map/aj,njk,bk->nab/dot_general | solution.py:13
  18.0 0.0 copy-done.1
  18.0 0.6 convolution_convert_fusion
  18.6 0.1 copy.12
  18.7 17.4 %all_gather.3 = bf16[1,256,1024]{2,1,0:T(8,128)(2,1)S(1)} all-gather(bf16[1,64,1024]{2,1,0:T(8,128)(2,1)S(1)} %copy.12), channel_id=1, replica_groups=mesh['grp'=2,'ex'=4,'lay'=4] {'ex'}, dimensions={1}, use_global_device_ids=true | all-gather | bytes 655360 | tf_op jit(solution)/shard_map/all_gather | solution.py:23
  36.1 4.5 %fusion.2 = bf16[256,2048]{1,0:T(8,128)(2,1)} fusion(bf16[1,2048,1024]{2,1,0:T(8,128)(2,1)} %param.5, bf16[1,256,1024]{2,1,0:T(8,128)(2,1)S(1)} %all_gather.3), kind=kOutput, calls=%fused_computation.2 | convolution fusion | flops 1074266112 | bytes 5767168 | tf_op jit(solution)/shard_map/lqf,ltf->qt/dot_general | solution.py:21
  40.6 0.0 reduce-scatter.2.cloned.1.call-update
  40.6 26.8 %reduce-scatter.2.cloned.1.call-done = bf16[256,512]{1,0:T(8,128)(2,1)} async-done(((bf16[256,2048]{1,0:T(8,128)(2,1)}), bf16[256,512]{1,0:T(8,128)(2,1)}) %reduce-scatter.2.cloned.1.call-update) | async-done | bytes 262160 | tf_op jit(solution)/shard_map/reduce_scatter | solution.py:27
Async XLA Ops:
  6.5 4.7 %copy-start = (f32[1,32,32]{2,1,0:T(8,128)S(1)}, f32[1,32,32]{2,1,0:T(8,128)}, u32[]{:S(2)}) copy-start(f32[1,32,32]{2,1,0:T(8,128)} %param.7) | copy-start | bytes 12292
  6.5 60.8 %reduce-scatter.2.cloned.1.call-start = ((), (), s32[]{:S(2)}) async-start(), calls=%async_computation.1 | async-start | bytes 1310720 | tf_op jit(solution)/shard_map/reduce_scatter | solution.py:27
  11.2 6.8 %copy-start.1 = (f32[1,32,32]{2,1,0:T(8,128)S(1)}, f32[1,32,32]{2,1,0:T(8,128)}, u32[]{:S(2)}) copy-start(f32[1,32,32]{2,1,0:T(8,128)} %param.8) | copy-start | bytes 12292
Sparse Core Ops, SparseCore 0:
  40.7 26.6 reduce-scatter.1
where the time goes:
time: 74.7 us; the launch traced here: 74.2 us
  waiting for transfers between devices  26.8 us (36%)
  blocking collectives  17.4 us (23%)
  between operations  14.1 us (19%)
  matrix products  11 us (15%)
  local copies, waits for them, and re-layouts  2.86 us (4%)
  other arithmetic  2.06 us (3%)
    reduce_scatter x1, waiting for transfers between devices, on_device(): lax.psum_scatter(block.astype(jnp.bfloat16), 'lay', scatter_dimension=1,...  26.8 us
    all_gather x1, blocking collectives, on_device(): lax.all_gather(conditioned, 'ex', axis=1, tiled=True)  17.4 us
    dot_general x1, matrix products, on_device(): jnp.einsum('lqf,ltf->qt', lax.all_gather(conditioned, 'ex', axis=1, tiled...  4.46 us
    dot_general x2, matrix products, condition(): jnp.einsum('aj,nab,bk->njk', out_mat, square, in_mat, precision=lax.Preci...  4.16 us
    dot_general x2, matrix products, condition(): jnp.einsum('aj,njk,bk->nab', out_mat, damped, in_mat, precision=lax.Preci...  2.38 us
  transfers between devices with their start and end apart: 1, of which 1 were waited for; matrix products, arithmetic and copies ran while one was open for 0% of the time, Pallas kernels for 0%

commit v1 on v0

v1 whole, which is shorter than its diff:
```python
import functools

import jax
import jax.numpy as jnp
from jax import lax
from jax.experimental import pallas as pl
from jax.experimental.pallas import tpu as pltpu
from jax.sharding import PartitionSpec as P

MESH = pl.DeviceIdType.MESH
F32 = jnp.float32
BF16 = jnp.bfloat16
PIECES = 2


def dot(a, b):
    return lax.dot_general(a, b, (((1,), (0,)), ((), ())), preferred_element_type=F32)


def dot_t(a, b):
    return lax.dot_general(a, b, (((1,), (1,)), ((), ())), preferred_element_type=F32)


def exact_dot(a, b):
    return jnp.dot(a, b, precision=lax.Precision.HIGHEST, preferred_element_type=F32)


def split(value):
    high = value.astype(BF16)
    return high, (value - high.astype(F32)).astype(BF16)


def kernel(
    n_ex, n_x,
    train_ref, query_ref, out_basis_ref, in_basis_ref, eigen_ref, scores_ref,
    train, held, out_mat, in_mat, eigen, wide_out, high, low, inverse,
    to_core, from_core, keep, to_chip, from_chip,
    local_sem, train_sem, gather_send, gather_recv, core_send, core_recv, chip_send, chip_recv,
):
    ex = lax.axis_index("ex")
    lay = lax.axis_index("lay")
    core = lax.rem(lay, 2)
    x = lax.div(lay, 2)
    n_lay = 2 * n_x
    width = train.shape[0] // n_lay
    count, flat = held.shape[1], held.shape[2]
    r_out, r_in = out_mat.shape[0], in_mat.shape[0]
    piece = count // PIECES
    middle = jnp.logical_and(ex > 0, ex < n_ex - 1)

    small = [
        pltpu.make_async_copy(out_basis_ref.at[0], out_mat, local_sem.at[0]),
        pltpu.make_async_copy(in_basis_ref.at[0], in_mat, local_sem.at[1]),
        pltpu.make_async_copy(eigen_ref.at[0], eigen, local_sem.at[2]),
        pltpu.make_async_copy(query_ref.at[0], held.at[ex], local_sem.at[3]),
    ]
    for copy in small:
        copy.start()

    barrier = pltpu.get_barrier_semaphore()

    @pl.when(ex > 0)
    def _():
        pl.semaphore_signal(barrier, inc=1, device_id={"ex": ex - 1}, device_id_type=MESH)

    @pl.when(ex < n_ex - 1)
    def _():
        pl.semaphore_signal(barrier, inc=1, device_id={"ex": ex + 1}, device_id_type=MESH)

    sibling = 2 * x + 1 - core
    pl.semaphore_signal(barrier, inc=1, device_id={"lay": sibling}, device_id_type=MESH)
    for step in range(1, n_x):
        other = lax.rem(x + step, n_x)
        pl.semaphore_signal(barrier, inc=1, device_id={"lay": 2 * other + core}, device_id_type=MESH)

    @pl.when(middle)
    def _():
        pl.semaphore_wait(barrier, n_x + 2)

    @pl.when(jnp.logical_not(middle))
    def _():
        pl.semaphore_wait(barrier, n_x + 1)

    def passing(shard, part, way, own=False):
        rows = pl.ds(part * piece, piece)
        return pltpu.make_async_remote_copy(
            src_ref=query_ref.at[0, rows] if own else held.at[shard, rows],
            dst_ref=held.at[shard, rows],
            send_sem=gather_send.at[way, shard, part],
            recv_sem=gather_recv.at[shard, part],
            device_id={"ex": ex + 2 * way - 1},
            device_id_type=MESH,
        )

    for part in range(PIECES):
        @pl.when(ex > 0)
        def _():
            passing(ex, part, 0, True).start()

        @pl.when(ex < n_ex - 1)
        def _():
            passing(ex, part, 1, True).start()

    blocks = [
        pltpu.make_async_copy(
            train_ref.at[0, pl.ds(g * width, width)], train.at[pl.ds(g * width, width)], train_sem.at[g]
        )
        for g in range(n_lay)
    ]
    for copy in blocks:
        copy.start()

    both = jnp.minimum(ex, n_ex - 1 - ex)

    def shard_of(step):
        near = lax.div(step + 1, 2)
        near_shard = jnp.where(lax.rem(step, 2) == 1, ex - near, ex + near)
        far = step - both
        far_shard = jnp.where(2 * ex < n_ex - 1, ex + far, ex - far)
        return jnp.where(step <= 2 * both, near_shard, far_shard)

    def arrive(step):
        shard = shard_of(step)
        for part in range(PIECES):
            passing(shard, part, 0).wait_recv()

            @pl.when(jnp.logical_and(shard > ex, ex > 0))
            def _():
                passing(shard, part, 0).start()

            @pl.when(jnp.logical_and(shard < ex, ex < n_ex - 1))
            def _():
                passing(shard, part, 1).start()

    for copy in small:
        copy.wait()
    column = lax.broadcasted_iota(jnp.int32, (r_in, flat), 1)
    inner = (lax.rem(column, r_in) == lax.broadcasted_iota(jnp.int32, (r_in, flat), 0)).astype(F32)
    outer_mask = lax.div(
        lax.broadcasted_iota(jnp.int32, (r_out, flat), 1), r_in
    ) == lax.broadcasted_iota(jnp.int32, (r_out, flat), 0)
    wide_out[...] = exact_dot(out_mat[...], outer_mask.astype(F32))
    wide_in = exact_dot(in_mat[...], inner)
    wide_eigen = exact_dot(eigen[...], inner)
    damping = 0.1 * jnp.mean(eigen[...])
    line = jnp.sum(jnp.where(outer_mask, wide_eigen, 0.0), axis=0, keepdims=True)
    inverse[...] = 1.0 / (line + damping)

    for a in range(r_out):
        above, below = split(wide_in * wide_out[a : a + 1, :])
        high[a * r_in : (a + 1) * r_in, :] = above
        low[a * r_in : (a + 1) * r_in, :] = below

    @pl.when(middle)
    def _():
        arrive(1)
        arrive(2)

    for copy in blocks:
        copy.wait()

    def core_copy(step):
        return pltpu.make_async_remote_copy(
            src_ref=to_core.at[step],
            dst_ref=from_core.at[step],
            send_sem=core_send.at[step],
            recv_sem=core_recv.at[step],
            device_id={"lay": sibling},
            device_id_type=MESH,
        )

    def chip_copy(step, other):
        return pltpu.make_async_remote_copy(
            src_ref=to_chip.at[step, other],
            dst_ref=from_chip.at[step, x],
            send_sem=chip_send.at[step, other],
            recv_sem=chip_recv.at[step, x],
            device_id={"lay": 2 * other + core},
            device_id_type=MESH,
        )

    def chip_arrival(step, other):
        return pltpu.make_async_remote_copy(
            src_ref=to_chip.at[step, other],
            dst_ref=from_chip.at[step, other],
            send_sem=chip_send.at[step, other],
            recv_sem=chip_recv.at[step, other],
            device_id={"lay": 2 * other + core},
            device_id_type=MESH,
        )

    def score(step):
        shard = shard_of(step)
        query = held[shard]
        rotated = dot(query, high[...]) + dot(query, low[...])
        above, below = split(rotated * inverse[...])
        conditioned = (
            dot_t(above, high[...]) + dot_t(below, high[...]) + dot_t(above, low[...])
        ).astype(BF16)
        for other in range(n_x):
            rows = pl.ds(pl.multiple_of((2 * other + 1 - core) * width, width), width)
            to_core[step, other] = dot_t(conditioned, train[rows, :]).astype(BF16)
        core_copy(step).start()
        for other in range(n_x):
            rows = pl.ds(pl.multiple_of((2 * other + core) * width, width), width)
            keep[step, other] = dot_t(conditioned, train[rows, :])

    def pair(step):
        core_copy(step).wait_recv()
        for hop in range(1, n_x):
            other = lax.rem(x + hop, n_x)
            to_chip[step, other] = (keep[step, other] + from_core[step, other].astype(F32)).astype(BF16)
            chip_copy(step, other).start()

    def finish(step):
        total = keep[step, x] + from_core[step, x].astype(F32)
        for hop in range(1, n_x):
            other = lax.rem(x + hop, n_x)
            chip_arrival(step, other).wait_recv()
            total += from_chip[step, other].astype(F32)
        rows = pl.ds(pl.multiple_of(shard_of(step) * count, count), count)
        scores_ref[rows, :] = total.astype(BF16)

    def turn(step, carry):
        @pl.when(jnp.logical_and(jnp.logical_not(middle), step >= 1))
        def _():
            arrive(step)

        @pl.when(jnp.logical_and(middle, jnp.logical_and(step >= 2, step < n_ex - 1)))
        def _():
            arrive(step + 1)

        score(step)

        @pl.when(step >= 1)
        def _():
            pair(step - 1)

        @pl.when(step >= 2)
        def _():
            finish(step - 2)

        return carry

    lax.fori_loop(0, n_ex, turn, 0)
    pair(n_ex - 1)
    if n_ex > 1:
        finish(n_ex - 2)
    finish(n_ex - 1)

    for part in range(PIECES):
        @pl.when(ex > 0)
        def _():
            passing(ex, part, 0, True).wait_send()

        @pl.when(ex < n_ex - 1)
        def _():
            passing(ex, part, 1, True).wait_send()

    def drain(step, carry):
        core_copy(step).wait_send()
        for hop in range(1, n_x):
            chip_copy(step, lax.rem(x + hop, n_x)).wait_send()

        @pl.when(step >= 1)
        def _():
            shard = shard_of(step)
            for part in range(PIECES):
                @pl.when(jnp.logical_and(shard > ex, ex > 0))
                def _():
                    passing(shard, part, 0).wait_send()

                @pl.when(jnp.logical_and(shard < ex, ex < n_ex - 1))
                def _():
                    passing(shard, part, 1).wait_send()

        return carry

    lax.fori_loop(0, n_ex, drain, 0)


def on_device(n_ex, n_lay, train_grads, queries, out_basis, in_basis, eigenvalues):
    n_x = n_lay // 2
    trains, flat = train_grads.shape[1:]
    count = queries.shape[1]
    width = trains // n_lay
    r_out, r_in = out_basis.shape[1], in_basis.shape[1]
    anywhere = pl.BlockSpec(memory_space=pl.ANY)
    dma = pltpu.SemaphoreType.DMA
    return pl.pallas_call(
        functools.partial(kernel, n_ex, n_x),
        out_shape=jax.ShapeDtypeStruct((n_ex * count, width), BF16),
        in_specs=[anywhere] * 5,
        out_specs=pl.BlockSpec(memory_space=pltpu.VMEM),
        scratch_shapes=[
            pltpu.VMEM((trains, flat), BF16),
            pltpu.VMEM((n_ex, count, flat), BF16),
            pltpu.VMEM((r_out, r_out), F32),
            pltpu.VMEM((r_in, r_in), F32),
            pltpu.VMEM((r_out, r_in), F32),
            pltpu.VMEM((r_out, flat), F32),
            pltpu.VMEM((flat, flat), BF16),
            pltpu.VMEM((flat, flat), BF16),
            pltpu.VMEM((1, flat), F32),
            pltpu.VMEM((n_ex, n_x, count, width), BF16),
            pltpu.VMEM((n_ex, n_x, count, width), BF16),
            pltpu.VMEM((n_ex, n_x, count, width), F32),
            pltpu.VMEM((n_ex, n_x, count, width), BF16),
            pltpu.VMEM((n_ex, n_x, count, width), BF16),
            dma((4,)),
            dma((n_lay,)),
            dma((2, n_ex, PIECES)),
            dma((n_ex, PIECES)),
            dma((n_ex,)),
            dma((n_ex,)),
            dma((n_ex, n_x)),
            dma((n_ex, n_x)),
        ],
        compiler_params=pltpu.CompilerParams(
            collective_id=0, has_side_effects=True, vmem_limit_bytes=56 * 1024 * 1024
        ),
        cost_estimate=pl.CostEstimate(
            flops=2 * n_ex * count * flat * (trains + 5 * flat),
            bytes_accessed=2 * (trains + count) * flat,
            transcendentals=0,
        ),
    )(train_grads, queries, out_basis, in_basis, eigenvalues)


def solution(mesh):
    placed = (
        P("lay", ("grp", "ex"), None),
        P("lay", ("grp", "ex"), None),
        P("lay", None, None),
        P("lay", None, None),
        P("lay", None, None),
    )
    return jax.shard_map(
        functools.partial(on_device, mesh.shape["ex"], mesh.shape["lay"]),
        mesh=mesh,
        in_specs=placed,
        out_specs=P("grp", ("ex", "lay")),
        check_vma=False,
    )
```

time: 74.7 us -> 33.3 us (0.45)
  Pallas kernels: 0 us -> 31.5 us
  waiting for transfers between devices: 26.8 us -> 0 us
  blocking collectives: 17.4 us -> 0 us
  between operations: 14.1 us -> 0.01 us
  matrix products: 11 us -> 0 us
  other arithmetic: 2.06 us -> 0 us
  local copies, waits for them, and re-layouts: 2.86 us -> 1.67 us
    pallas_call x0 -> x1, Pallas kernels: none -> 31.5 us  [on_device(): pl.pallas_call(functools.partial(kernel, n_ex, n_x), out_shape=jax.ShapeD...]
    reduce_scatter x1 -> x0, waiting for transfers between devices: 26.8 us -> none  [on_device(): lax.psum_scatter(block.astype(jnp.bfloat16), 'lay', scatter_dimension=1,...]
    all_gather x1 -> x0, blocking collectives: 17.4 us -> none  [on_device(): lax.all_gather(conditioned, 'ex', axis=1, tiled=True)]
    dot_general x5 -> x0, matrix products: 11 us -> none  [the longest x1 4.46 us: on_device(): jnp.einsum('lqf,ltf->qt', lax.all_gather(conditioned, 'ex', axis=1, tiled...]
    reduce_sum x1 -> x0, other arithmetic: 1.34 us -> none  [condition(): damping = 0.1 * jnp.mean(eigen)]
    reshape x1 -> x0, local copies, waits for them, and re-layouts: 0.88 us -> none  [condition(): grads.astype(jnp.float32).reshape(count, out_mat.shape[0], in_mat.shape[0])]
    dot_general x1 -> x0, local copies, waits for them, and re-layouts: 0.77 us -> none  [condition(): jnp.einsum('aj,njk,bk->nab', out_mat, damped, in_mat, precision=lax.Preci...]
    unnamed x5 -> x1, local copies, waits for them, and re-layouts: 1.08 us -> 1.67 us
  transfers between devices with their start and end apart: 1 -> 0, of which waited for: 1 -> 0; matrix products, arithmetic and copies ran while one was open for 0% -> 0% of each run, Pallas kernels for 0% -> 0%
where the time goes in v1:
time: 33.3 us; the launch traced here: 33.2 us
  Pallas kernels  31.5 us (95%)
  local copies, waits for them, and re-layouts  1.67 us (5%)
    pallas_call x1, Pallas kernels, on_device(): pl.pallas_call(functools.partial(kernel, n_ex, n_x), out_shape=jax.ShapeD...  31.5 us
    unnamed x1, local copies, waits for them, and re-layouts  1.67 us

profile of v1, /device:TPU:0, one launch (start us, length us, event | category | flops | bytes accessed | tf_op | source)
XLA Modules:
  0.0 33.2 jit_solution(17892629324523865280)
XLA Ops:
  0.0 31.5 %shard_map.55 = bf16[256,512]{1,0:T(8,128)(2,1)} custom-call(bf16[1,2048,1024]{2,1,0:T(8,128)(2,1)} %train_ref.1, bf16[1,64,1024]{2,1,0:T(8,128)(2,1)} %query_ref.1, f32[1,32,32]{2,1,0:T(8,128)} %out_basis_ref.1, f32[1,32,32]{2,1,0:T(8,128)} %in_basis_ref.1, f32[1,32,32]{2,1,0:T(8,128)} %eigen_ref.1), custom_call_target="tpu_custom_call" | custom-call | flops 3758096384 | bytes 4325376 | tf_op jit(solution)/shard_map/pallas_call | solution.py:290
  31.5 1.7 %copy.7 = bf16[256,512]{1,0:T(8,128)(2,1)} copy(bf16[256,512]{1,0:T(8,128)(2,1)} %shard_map.55) | data formatting | bytes 524288

commit v2 on v1

--- a/solution.py
+++ b/solution.py
@@ -17,10 +17,6 @@
     return lax.dot_general(a, b, (((1,), (0,)), ((), ())), preferred_element_type=F32)
 
 
-def dot_t(a, b):
-    return lax.dot_general(a, b, (((1,), (1,)), ((), ())), preferred_element_type=F32)
-
-
 def exact_dot(a, b):
     return jnp.dot(a, b, precision=lax.Precision.HIGHEST, preferred_element_type=F32)
 
@@ -33,7 +29,7 @@
 def kernel(
     n_ex, n_x,
     train_ref, query_ref, out_basis_ref, in_basis_ref, eigen_ref, scores_ref,
-    train, held, out_mat, in_mat, eigen, wide_out, high, low, inverse,
+    train, train_t, held, out_mat, in_mat, eigen, wide_out, high, low, high_t, low_t, inverse,
     to_core, from_core, keep, to_chip, from_chip,
     local_sem, train_sem, gather_send, gather_recv, core_send, core_recv, chip_send, chip_recv,
 ):
@@ -139,25 +135,36 @@
     outer_mask = lax.div(
         lax.broadcasted_iota(jnp.int32, (r_out, flat), 1), r_in
     ) == lax.broadcasted_iota(jnp.int32, (r_out, flat), 0)
-    wide_out[...] = exact_dot(out_mat[...], outer_mask.astype(F32))
-    wide_in = exact_dot(in_mat[...], inner)
+    outer = outer_mask.astype(F32)
     wide_eigen = exact_dot(eigen[...], inner)
     damping = 0.1 * jnp.mean(eigen[...])
     line = jnp.sum(jnp.where(outer_mask, wide_eigen, 0.0), axis=0, keepdims=True)
     inverse[...] = 1.0 / (line + damping)
 
-    for a in range(r_out):
-        above, below = split(wide_in * wide_out[a : a + 1, :])
-        high[a * r_in : (a + 1) * r_in, :] = above
-        low[a * r_in : (a + 1) * r_in, :] = below
+    def spread(out_part, in_part, above_ref, below_ref):
+        wide_out[...] = exact_dot(out_part, outer)
+        wide_in = exact_dot(in_part, inner)
+        for a in range(r_out):
+            above, below = split(wide_in * wide_out[a : a + 1, :])
+            above_ref[a * r_in : (a + 1) * r_in, :] = above
+            below_ref[a * r_in : (a + 1) * r_in, :] = below
+
+    spread(out_mat[...], in_mat[...], high, low)
+    spread(out_mat[...].T, in_mat[...].T, high_t, low_t)
 
     @pl.when(middle)
     def _():
         arrive(1)
         arrive(2)
 
-    for copy in blocks:
+    for g, copy in enumerate(blocks):
         copy.wait()
+        span = slice(g * width, (g + 1) * width)
+        train_t[:, span] = train[span, :].T
+
+    @pl.when(jnp.logical_not(middle))
+    def _():
+        arrive(1)
 
     def core_copy(step):
         return pltpu.make_async_remote_copy(
@@ -189,21 +196,28 @@
             device_id_type=MESH,
         )
 
-    def score(step):
-        shard = shard_of(step)
-        query = held[shard]
+    def score(steps):
+        query = jnp.concatenate([held[shard_of(step)] for step in steps], axis=0)
         rotated = dot(query, high[...]) + dot(query, low[...])
         above, below = split(rotated * inverse[...])
-        conditioned = (
-            dot_t(above, high[...]) + dot_t(below, high[...]) + dot_t(above, low[...])
-        ).astype(BF16)
+        stacked = dot(jnp.concatenate([above, below], axis=0), high_t[...])
+        rows = query.shape[0]
+        conditioned = (stacked[:rows] + stacked[rows:] + dot(above, low_t[...])).astype(BF16)
+
+        def block(g):
+            start = pl.multiple_of(g * width, width)
+            return dot(conditioned, train_t[:, pl.ds(start, width)])
+
         for other in range(n_x):
-            rows = pl.ds(pl.multiple_of((2 * other + 1 - core) * width, width), width)
-            to_core[step, other] = dot_t(conditioned, train[rows, :]).astype(BF16)
-        core_copy(step).start()
+            part = block(2 * other + 1 - core).astype(BF16)
+            for at, step in enumerate(steps):
+                to_core[step, other] = part[at * count : (at + 1) * count]
+        for step in steps:
+            core_copy(step).start()
         for other in range(n_x):
-            rows = pl.ds(pl.multiple_of((2 * other + core) * width, width), width)
-            keep[step, other] = dot_t(conditioned, train[rows, :])
+            part = block(2 * other + core)
+            for at, step in enumerate(steps):
+                keep[step, other] = part[at * count : (at + 1) * count]
 
     def pair(step):
         core_copy(step).wait_recv()
@@ -222,30 +236,24 @@
         scores_ref[rows, :] = total.astype(BF16)
 
     def turn(step, carry):
-        @pl.when(jnp.logical_and(jnp.logical_not(middle), step >= 1))
+        @pl.when(jnp.logical_not(middle))
         def _():
             arrive(step)
 
-        @pl.when(jnp.logical_and(middle, jnp.logical_and(step >= 2, step < n_ex - 1)))
+        @pl.when(jnp.logical_and(middle, step < n_ex - 1))
         def _():
             arrive(step + 1)
 
-        score(step)
-
-        @pl.when(step >= 1)
-        def _():
-            pair(step - 1)
-
-        @pl.when(step >= 2)
-        def _():
-            finish(step - 2)
-
+        score((step,))
+        pair(step)
+        finish(step - 1)
         return carry
 
-    lax.fori_loop(0, n_ex, turn, 0)
-    pair(n_ex - 1)
-    if n_ex > 1:
-        finish(n_ex - 2)
+    score((0, 1))
+    pair(0)
+    pair(1)
+    finish(0)
+    lax.fori_loop(2, n_ex, turn, 0)
     finish(n_ex - 1)
 
     for part in range(PIECES):
@@ -294,11 +302,14 @@
         out_specs=pl.BlockSpec(memory_space=pltpu.VMEM),
         scratch_shapes=[
             pltpu.VMEM((trains, flat), BF16),
+            pltpu.VMEM((flat, trains), BF16),
             pltpu.VMEM((n_ex, count, flat), BF16),
             pltpu.VMEM((r_out, r_out), F32),
             pltpu.VMEM((r_in, r_in), F32),
             pltpu.VMEM((r_out, r_in), F32),
             pltpu.VMEM((r_out, flat), F32),
+            pltpu.VMEM((flat, flat), BF16),
+            pltpu.VMEM((flat, flat), BF16),
             pltpu.VMEM((flat, flat), BF16),
             pltpu.VMEM((flat, flat), BF16),
             pltpu.VMEM((1, flat), F32),

time: 33.3 us -> 31 us (0.931)
  Pallas kernels: 31.5 us -> 29.1 us
    pallas_call x1, Pallas kernels: 31.5 us -> 29.1 us  [on_device(): pl.pallas_call(functools.partial(kernel, n_ex, n_x), out_shape=jax.ShapeD...]
where the time goes in v2:
time: 31 us; the launch traced here: 30.8 us
  Pallas kernels  29.1 us (94%)
  local copies, waits for them, and re-layouts  1.67 us (5%)
    pallas_call x1, Pallas kernels, on_device(): pl.pallas_call(functools.partial(kernel, n_ex, n_x), out_shape=jax.ShapeD...  29.1 us
    unnamed x1, local copies, waits for them, and re-layouts  1.67 us

profile of v2, /device:TPU:0, one launch (start us, length us, event | category | flops | bytes accessed | tf_op | source)
XLA Modules:
  0.0 30.8 jit_solution(6416118651821962271)
XLA Ops:
  0.0 29.1 %shard_map.55 = bf16[256,512]{1,0:T(8,128)(2,1)} custom-call(bf16[1,2048,1024]{2,1,0:T(8,128)(2,1)} %train_ref.1, bf16[1,64,1024]{2,1,0:T(8,128)(2,1)} %query_ref.1, f32[1,32,32]{2,1,0:T(8,128)} %out_basis_ref.1, f32[1,32,32]{2,1,0:T(8,128)} %in_basis_ref.1, f32[1,32,32]{2,1,0:T(8,128)} %eigen_ref.1), custom_call_target="tpu_custom_call" | custom-call | flops 3758096384 | bytes 4325376 | tf_op jit(solution)/shard_map/pallas_call | solution.py:298
  29.2 1.7 %copy.7 = bf16[256,512]{1,0:T(8,128)(2,1)} copy(bf16[256,512]{1,0:T(8,128)(2,1)} %shard_map.55) | data formatting | bytes 524288

commit v3 on v2

--- a/solution.py
+++ b/solution.py
@@ -17,6 +17,10 @@
     return lax.dot_general(a, b, (((1,), (0,)), ((), ())), preferred_element_type=F32)
 
 
+def dot_t(a, b):
+    return lax.dot_general(a, b, (((1,), (1,)), ((), ())), preferred_element_type=F32)
+
+
 def exact_dot(a, b):
     return jnp.dot(a, b, precision=lax.Precision.HIGHEST, preferred_element_type=F32)
 
@@ -29,7 +33,7 @@
 def kernel(
     n_ex, n_x,
     train_ref, query_ref, out_basis_ref, in_basis_ref, eigen_ref, scores_ref,
-    train, train_t, held, out_mat, in_mat, eigen, wide_out, high, low, high_t, low_t, inverse,
+    train, held, out_mat, in_mat, eigen, wide_out, product, product_t, inverse,
     to_core, from_core, keep, to_chip, from_chip,
     local_sem, train_sem, gather_send, gather_recv, core_send, core_recv, chip_send, chip_recv,
 ):
@@ -141,26 +145,22 @@
     line = jnp.sum(jnp.where(outer_mask, wide_eigen, 0.0), axis=0, keepdims=True)
     inverse[...] = 1.0 / (line + damping)
 
-    def spread(out_part, in_part, above_ref, below_ref):
+    def spread(out_part, in_part, target):
         wide_out[...] = exact_dot(out_part, outer)
         wide_in = exact_dot(in_part, inner)
         for a in range(r_out):
-            above, below = split(wide_in * wide_out[a : a + 1, :])
-            above_ref[a * r_in : (a + 1) * r_in, :] = above
-            below_ref[a * r_in : (a + 1) * r_in, :] = below
-
-    spread(out_mat[...], in_mat[...], high, low)
-    spread(out_mat[...].T, in_mat[...].T, high_t, low_t)
+            target[a * r_in : (a + 1) * r_in, :] = (wide_in * wide_out[a : a + 1, :]).astype(BF16)
+
+    spread(out_mat[...], in_mat[...], product)
+    spread(out_mat[...].T, in_mat[...].T, product_t)
 
     @pl.when(middle)
     def _():
         arrive(1)
         arrive(2)
 
-    for g, copy in enumerate(blocks):
+    for copy in blocks:
         copy.wait()
-        span = slice(g * width, (g + 1) * width)
-        train_t[:, span] = train[span, :].T
 
     @pl.when(jnp.logical_not(middle))
     def _():
@@ -198,15 +198,15 @@
 
     def score(steps):
         query = jnp.concatenate([held[shard_of(step)] for step in steps], axis=0)
-        rotated = dot(query, high[...]) + dot(query, low[...])
+        rotated = dot(query, product[...])
         above, below = split(rotated * inverse[...])
-        stacked = dot(jnp.concatenate([above, below], axis=0), high_t[...])
+        stacked = dot(jnp.concatenate([above, below], axis=0), product_t[...])
         rows = query.shape[0]
-        conditioned = (stacked[:rows] + stacked[rows:] + dot(above, low_t[...])).astype(BF16)
+        conditioned = (stacked[:rows] + stacked[rows:]).astype(BF16)
 
         def block(g):
             start = pl.multiple_of(g * width, width)
-            return dot(conditioned, train_t[:, pl.ds(start, width)])
+            return dot_t(conditioned, train[pl.ds(start, width), :])
 
         for other in range(n_x):
             part = block(2 * other + 1 - core).astype(BF16)
@@ -302,14 +302,11 @@
         out_specs=pl.BlockSpec(memory_space=pltpu.VMEM),
         scratch_shapes=[
             pltpu.VMEM((trains, flat), BF16),
-            pltpu.VMEM((flat, trains), BF16),
             pltpu.VMEM((n_ex, count, flat), BF16),
             pltpu.VMEM((r_out, r_out), F32),
             pltpu.VMEM((r_in, r_in), F32),
             pltpu.VMEM((r_out, r_in), F32),
             pltpu.VMEM((r_out, flat), F32),
-            pltpu.VMEM((flat, flat), BF16),
-            pltpu.VMEM((flat, flat), BF16),
             pltpu.VMEM((flat, flat), BF16),
             pltpu.VMEM((flat, flat), BF16),
             pltpu.VMEM((1, flat), F32),
@@ -331,7 +328,7 @@
             collective_id=0, has_side_effects=True, vmem_limit_bytes=56 * 1024 * 1024
         ),
         cost_estimate=pl.CostEstimate(
-            flops=2 * n_ex * count * flat * (trains + 5 * flat),
+            flops=2 * n_ex * count * flat * (trains + 3 * flat),
             bytes_accessed=2 * (trains + count) * flat,
             transcendentals=0,
         ),

time: 31 us -> 28.7 us (0.926)
  Pallas kernels: 29.1 us -> 26.9 us
    pallas_call x1, Pallas kernels: 29.1 us -> 26.9 us  [on_device(): pl.pallas_call(functools.partial(kernel, n_ex, n_x), out_shape=jax.ShapeD...]
where the time goes in v3:
time: 28.7 us; the launch traced here: 28.6 us
  Pallas kernels  26.9 us (94%)
  local copies, waits for them, and re-layouts  1.67 us (6%)
    pallas_call x1, Pallas kernels, on_device(): pl.pallas_call(functools.partial(kernel, n_ex, n_x), out_shape=jax.ShapeD...  26.9 us
    unnamed x1, local copies, waits for them, and re-layouts  1.67 us

profile of v3, /device:TPU:0, one launch (start us, length us, event | category | flops | bytes accessed | tf_op | source)
XLA Modules:
  0.0 28.6 jit_solution(7054187739808867659)
XLA Ops:
  0.0 26.9 %shard_map.55 = bf16[256,512]{1,0:T(8,128)(2,1)} custom-call(bf16[1,2048,1024]{2,1,0:T(8,128)(2,1)} %train_ref.1, bf16[1,64,1024]{2,1,0:T(8,128)(2,1)} %query_ref.1, f32[1,32,32]{2,1,0:T(8,128)} %out_basis_ref.1, f32[1,32,32]{2,1,0:T(8,128)} %in_basis_ref.1, f32[1,32,32]{2,1,0:T(8,128)} %eigen_ref.1), custom_call_target="tpu_custom_call" | custom-call | flops 2684354560 | bytes 4325376 | tf_op jit(solution)/shard_map/pallas_call | solution.py:298
  26.9 1.7 %copy.7 = bf16[256,512]{1,0:T(8,128)(2,1)} copy(bf16[256,512]{1,0:T(8,128)(2,1)} %shard_map.55) | data formatting | bytes 524288

commit v4 on v3

--- a/solution.py
+++ b/solution.py
@@ -166,12 +166,12 @@
     def _():
         arrive(1)
 
-    def core_copy(step):
+    def core_copy(step, other):
         return pltpu.make_async_remote_copy(
-            src_ref=to_core.at[step],
-            dst_ref=from_core.at[step],
-            send_sem=core_send.at[step],
-            recv_sem=core_recv.at[step],
+            src_ref=to_core.at[step, other],
+            dst_ref=from_core.at[step, other],
+            send_sem=core_send.at[step, other],
+            recv_sem=core_recv.at[step, other],
             device_id={"lay": sibling},
             device_id_type=MESH,
         )
@@ -208,25 +208,36 @@
             start = pl.multiple_of(g * width, width)
             return dot_t(conditioned, train[pl.ds(start, width), :])
 
-        for other in range(n_x):
+        def give(other):
             part = block(2 * other + 1 - core).astype(BF16)
             for at, step in enumerate(steps):
                 to_core[step, other] = part[at * count : (at + 1) * count]
-        for step in steps:
-            core_copy(step).start()
-        for other in range(n_x):
+            for step in steps:
+                core_copy(step, other).start()
+
+        def hold(other):
             part = block(2 * other + core)
             for at, step in enumerate(steps):
                 keep[step, other] = part[at * count : (at + 1) * count]
 
+        for hop in range(1, n_x):
+            give(lax.rem(x + hop, n_x))
+        for hop in range(1, n_x):
+            hold(lax.rem(x + hop, n_x))
+        give(x)
+        for step in steps:
+            pair(step)
+        hold(x)
+
     def pair(step):
-        core_copy(step).wait_recv()
         for hop in range(1, n_x):
             other = lax.rem(x + hop, n_x)
+            core_copy(step, other).wait_recv()
             to_chip[step, other] = (keep[step, other] + from_core[step, other].astype(F32)).astype(BF16)
             chip_copy(step, other).start()
 
     def finish(step):
+        core_copy(step, x).wait_recv()
         total = keep[step, x] + from_core[step, x].astype(F32)
         for hop in range(1, n_x):
             other = lax.rem(x + hop, n_x)
@@ -245,13 +256,10 @@
             arrive(step + 1)
 
         score((step,))
-        pair(step)
         finish(step - 1)
         return carry
 
     score((0, 1))
-    pair(0)
-    pair(1)
     finish(0)
     lax.fori_loop(2, n_ex, turn, 0)
     finish(n_ex - 1)
@@ -266,9 +274,11 @@
             passing(ex, part, 1, True).wait_send()
 
     def drain(step, carry):
-        core_copy(step).wait_send()
-        for hop in range(1, n_x):
-            chip_copy(step, lax.rem(x + hop, n_x)).wait_send()
+        core_copy(step, x).wait_send()
+        for hop in range(1, n_x):
+            other = lax.rem(x + hop, n_x)
+            core_copy(step, other).wait_send()
+            chip_copy(step, other).wait_send()
 
         @pl.when(step >= 1)
         def _():
@@ -319,8 +329,8 @@
             dma((n_lay,)),
             dma((2, n_ex, PIECES)),
             dma((n_ex, PIECES)),
-            dma((n_ex,)),
-            dma((n_ex,)),
+            dma((n_ex, n_x)),
+            dma((n_ex, n_x)),
             dma((n_ex, n_x)),
             dma((n_ex, n_x)),
         ],

time: 28.7 us -> 27.9 us (0.972)
  Pallas kernels: 26.9 us -> 26.1 us
    pallas_call x1, Pallas kernels: 26.9 us -> 26.1 us  [on_device(): pl.pallas_call(functools.partial(kernel, n_ex, n_x), out_shape=jax.ShapeD...]
where the time goes in v4:
time: 27.9 us; the launch traced here: 27.7 us
  Pallas kernels  26.1 us (94%)
  local copies, waits for them, and re-layouts  1.67 us (6%)
    pallas_call x1, Pallas kernels, on_device(): pl.pallas_call(functools.partial(kernel, n_ex, n_x), out_shape=jax.ShapeD...  26.1 us
    unnamed x1, local copies, waits for them, and re-layouts  1.67 us

profile of v4, /device:TPU:0, one launch (start us, length us, event | category | flops | bytes accessed | tf_op | source)
XLA Modules:
  0.0 27.7 jit_solution(17632214295109786785)
XLA Ops:
  0.0 26.1 %shard_map.55 = bf16[256,512]{1,0:T(8,128)(2,1)} custom-call(bf16[1,2048,1024]{2,1,0:T(8,128)(2,1)} %train_ref.1, bf16[1,64,1024]{2,1,0:T(8,128)(2,1)} %query_ref.1, f32[1,32,32]{2,1,0:T(8,128)} %out_basis_ref.1, f32[1,32,32]{2,1,0:T(8,128)} %in_basis_ref.1, f32[1,32,32]{2,1,0:T(8,128)} %eigen_ref.1), custom_call_target="tpu_custom_call" | custom-call | flops 2684354560 | bytes 4325376 | tf_op jit(solution)/shard_map/pallas_call | solution.py:308
  26.1 1.7 %copy.7 = bf16[256,512]{1,0:T(8,128)(2,1)} copy(bf16[256,512]{1,0:T(8,128)(2,1)} %shard_map.55) | data formatting | bytes 524288

commit v5 on v4

--- a/solution.py
+++ b/solution.py
@@ -34,7 +34,7 @@
     n_ex, n_x,
     train_ref, query_ref, out_basis_ref, in_basis_ref, eigen_ref, scores_ref,
     train, held, out_mat, in_mat, eigen, wide_out, product, product_t, inverse,
-    to_core, from_core, keep, to_chip, from_chip,
+    to_core, from_core, keep, to_chip, from_chip, result, result_sem,
     local_sem, train_sem, gather_send, gather_recv, core_send, core_recv, chip_send, chip_recv,
 ):
     ex = lax.axis_index("ex")
@@ -236,6 +236,10 @@
             to_chip[step, other] = (keep[step, other] + from_core[step, other].astype(F32)).astype(BF16)
             chip_copy(step, other).start()
 
+    def result_copy(step):
+        rows = pl.ds(pl.multiple_of(shard_of(step) * count, count), count)
+        return pltpu.make_async_copy(result.at[rows], scores_ref.at[rows], result_sem.at[step])
+
     def finish(step):
         core_copy(step, x).wait_recv()
         total = keep[step, x] + from_core[step, x].astype(F32)
@@ -244,7 +248,8 @@
             chip_arrival(step, other).wait_recv()
             total += from_chip[step, other].astype(F32)
         rows = pl.ds(pl.multiple_of(shard_of(step) * count, count), count)
-        scores_ref[rows, :] = total.astype(BF16)
+        result[rows, :] = total.astype(BF16)
+        result_copy(step).start()
 
     def turn(step, carry):
         @pl.when(jnp.logical_not(middle))
@@ -274,6 +279,7 @@
             passing(ex, part, 1, True).wait_send()
 
     def drain(step, carry):
+        result_copy(step).wait()
         core_copy(step, x).wait_send()
         for hop in range(1, n_x):
             other = lax.rem(x + hop, n_x)
@@ -309,7 +315,7 @@
         functools.partial(kernel, n_ex, n_x),
         out_shape=jax.ShapeDtypeStruct((n_ex * count, width), BF16),
         in_specs=[anywhere] * 5,
-        out_specs=pl.BlockSpec(memory_space=pltpu.VMEM),
+        out_specs=anywhere,
         scratch_shapes=[
             pltpu.VMEM((trains, flat), BF16),
             pltpu.VMEM((n_ex, count, flat), BF16),
@@ -325,6 +331,8 @@
             pltpu.VMEM((n_ex, n_x, count, width), F32),
             pltpu.VMEM((n_ex, n_x, count, width), BF16),
             pltpu.VMEM((n_ex, n_x, count, width), BF16),
+            pltpu.VMEM((n_ex * count, width), BF16),
+            dma((n_ex,)),
             dma((4,)),
             dma((n_lay,)),
             dma((2, n_ex, PIECES)),

time: 27.9 us -> 27.7 us (level)
  no operation moved by 1% of the time
where the time goes in v5:
time: 27.7 us; the launch traced here: 27.6 us
  Pallas kernels  25.9 us (94%)
  local copies, waits for them, and re-layouts  1.67 us (6%)
    pallas_call x1, Pallas kernels, on_device(): pl.pallas_call(functools.partial(kernel, n_ex, n_x), out_shape=jax.ShapeD...  25.9 us
    unnamed x1, local copies, waits for them, and re-layouts  1.67 us

profile of v5, /device:TPU:0, one launch (start us, length us, event | category | flops | bytes accessed | tf_op | source)
XLA Modules:
  0.0 27.6 jit_solution(18239931103581072274)
XLA Ops:
  0.0 25.9 %shard_map.55 = bf16[256,512]{1,0:T(8,128)(2,1)} custom-call(bf16[1,2048,1024]{2,1,0:T(8,128)(2,1)} %train_ref.1, bf16[1,64,1024]{2,1,0:T(8,128)(2,1)} %query_ref.1, f32[1,32,32]{2,1,0:T(8,128)} %out_basis_ref.1, f32[1,32,32]{2,1,0:T(8,128)} %in_basis_ref.1, f32[1,32,32]{2,1,0:T(8,128)} %eigen_ref.1), custom_call_target="tpu_custom_call" | custom-call | flops 2684354560 | bytes 4325376 | tf_op jit(solution)/shard_map/pallas_call | solution.py:314
  25.9 1.7 %copy.7 = bf16[256,512]{1,0:T(8,128)(2,1)} copy(bf16[256,512]{1,0:T(8,128)(2,1)} %shard_map.55) | data formatting | bytes 524288
